TPU v7x, 32 devices: a whole 2x2x4 slice. The times are simulated.
32 devices in a mesh: dp: 16 (over z, y, core), tensor: 2 (over x).
Axes of the slice: x: 2, y: 2, z: 4, core: 2. Of those that a mesh axis runs over, the one named last changes fastest.
Arguments:
- tokens: bfloat16 [24000, 512], P(('dp', 'tensor')), may hold values from -16 to 16
- ff_in: bfloat16 [1, 2, 512, 2048], P(None, None, None, ('dp', 'tensor')), may hold values from -0.25 to 0.25
- ff_out: bfloat16 [1, 2, 2048, 512], P(None, None, ('dp', 'tensor')), may hold values from -0.25 to 0.25
- att_qkv: bfloat16 [1, 512, 3, 512], P(None, 'dp', None, 'tensor'), may hold values from -0.25 to 0.25
- att_pos: bfloat16 [1, 512, 512], P(None, 'dp', 'tensor'), may hold values from -0.25 to 0.25
- att_bias: bfloat16 [1, 8, 128], P(None, 'tensor', 'dp'), may hold values from -3 to 3
- att_out: bfloat16 [1, 512, 512], P(None, 'tensor', 'dp'), may hold values from -1 to 1
- conv_in: bfloat16 [1, 512, 2, 512], P(None, None, None, ('dp', 'tensor')), may hold values from -0.25 to 0.25
- conv_depth: bfloat16 [1, 31, 512], P(None, None, ('dp', 'tensor')), may hold values from -1 to 1
- conv_out: bfloat16 [1, 512, 512], P(None, ('dp', 'tensor')), may hold values from -0.25 to 0.25
- gains: float32 [1, 7, 512], P(None, None, ('dp', 'tensor')), may hold values from 0.1 to 1.9
- out_grad: float32 [24000, 512], P(('dp', 'tensor')), may hold values from -6 to 6
Outputs:
- block_out: float32 [24000, 512], P(('dp', 'tensor'))
- tokens_grad: float32 [24000, 512], P(('dp', 'tensor'))
- ff_in_grad: float32 [1, 2, 512, 2048], P(None, None, None, ('dp', 'tensor'))
- ff_out_grad: float32 [1, 2, 2048, 512], P(None, None, ('dp', 'tensor'))
- att_qkv_grad: float32 [1, 512, 3, 512], P(None, 'dp', None, 'tensor')
- att_pos_grad: float32 [1, 512, 512], P(None, 'dp', 'tensor')
- att_bias_grad: float32 [1, 8, 128], P(None, 'tensor', 'dp')
- att_out_grad: float32 [1, 512, 512], P(None, 'tensor', 'dp')
- conv_in_grad: float32 [1, 512, 2, 512], P(None, None, None, ('dp', 'tensor'))
- conv_depth_grad: float32 [1, 31, 512], P(None, None, ('dp', 'tensor'))
- conv_out_grad: float32 [1, 512, 512], P(None, ('dp', 'tensor'))
- gains_grad: float32 [1, 7, 512], P(None, None, ('dp', 'tensor'))
All inputs are finite; a program needn't handle non-finite values.
Results may differ from a plain program's by a relative error of at most 0.028.
Values may be sent and summed in bfloat16 or wider, within the bound.
A program may use at most 256 MiB of HBM per device.

v0:
```python
import math

import jax
import jax.numpy as jnp
from jax import lax
from jax.experimental import pallas as pl
from jax.experimental.pallas import tpu as pltpu
from jax.sharding import PartitionSpec as P

DH = 64
EPS = 1e-05
AXES = ("dp", "tensor")
BLOCK = 128
PAIR = 128
F32 = jnp.float32
BF16 = jnp.bfloat16


def matmul(left, right):
    return jnp.dot(left, right, preferred_element_type=F32)


def inner_rows(left, right):
    return lax.dot_general(left, right, (((0,), (0,)), ((), ())), preferred_element_type=F32)


def outer_cols(left, right):
    return lax.dot_general(left, right, (((1,), (1,)), ((), ())), preferred_element_type=F32)


def norm_parts(inputs):
    centre = inputs - jnp.mean(inputs, axis=-1, keepdims=True)
    inverse = lax.rsqrt(jnp.mean(centre * centre, axis=-1, keepdims=True) + EPS)
    return centre * inverse, inverse


def layer_norm(inputs, gain):
    return norm_parts(inputs)[0] * gain


def norm_back(inputs, gain, upstream):
    unit, inverse = norm_parts(inputs)
    scaled = upstream * gain
    mean_scaled = jnp.mean(scaled, axis=-1, keepdims=True)
    mean_product = jnp.mean(scaled * unit, axis=-1, keepdims=True)
    grad = inverse * (scaled - mean_scaled - unit * mean_product)
    return grad, jnp.sum(upstream * unit, axis=0)


def silu_slope(values):
    gate = jax.nn.sigmoid(values)
    return gate * (1.0 + values * (1.0 - gate))


def head_mask(head, scale):
    lanes = lax.broadcasted_iota(jnp.int32, (1, PAIR), 1)
    return jnp.where(lanes // DH == head, scale, 0.0).astype(BF16)


def padded_table(padded, model_width):
    distance = (padded - 1 - lax.broadcasted_iota(jnp.int32, (2 * padded, 1), 0)).astype(F32)
    columns = lax.broadcasted_iota(jnp.int32, (1, model_width), 1)
    frequency = jnp.exp((columns // 2).astype(F32) * (-2.0 * math.log(10000.0) / model_width))
    angles = distance * frequency
    return jnp.where(columns % 2 == 0, jnp.sin(angles), jnp.cos(angles)).astype(BF16)


def attend_forward(query_a, query_b, key_rows, value_rows, pos_keys, length):
    padded, width = key_rows.shape
    span = padded + BLOCK

    def kernel(qa_ref, qb_ref, k_ref, v_ref, pk_ref, out_ref, probs_ref):
        columns = lax.broadcasted_iota(jnp.int32, (BLOCK, padded), 1)

        def one_block(block, carry):
            rows = pl.ds(pl.multiple_of(block * BLOCK, BLOCK), BLOCK)
            near = pl.ds(pl.multiple_of(padded - BLOCK - block * BLOCK, BLOCK), span)
            total = jnp.zeros((BLOCK, PAIR), F32)
            for head in range(2):
                scale = head_mask(head, DH ** (-0.5))
                content = outer_cols(qa_ref[rows, :] * scale, k_ref[...])
                position = outer_cols(qb_ref[rows, :] * scale, pk_ref[near, :])
                position = pltpu.roll(
                    position, span - BLOCK + 1, 1, stride=1, stride_axis=0
                )[:, :padded]
                scores = jnp.where(columns < length, content + position, -1e30)
                weights = jnp.exp(scores - jnp.max(scores, axis=-1, keepdims=True))
                inverse = 1.0 / jnp.sum(weights, axis=-1, keepdims=True)
                probs = (weights * inverse).astype(BF16)
                probs_ref[head, rows, :] = probs
                total += matmul(probs, v_ref[...] * head_mask(head, 1.0))
            out_ref[rows, :] = total.astype(BF16)
            return carry

        lax.fori_loop(0, padded // BLOCK, one_block, 0)

    rows_spec = pl.BlockSpec((padded, PAIR), lambda pair: (0, pair))
    return pl.pallas_call(
        kernel,
        grid=(width // PAIR,),
        in_specs=[rows_spec] * 4 + [pl.BlockSpec((2 * padded, PAIR), lambda pair: (0, pair))],
        out_specs=[rows_spec, pl.BlockSpec((2, padded, padded), lambda pair: (pair, 0, 0))],
        out_shape=[
            jax.ShapeDtypeStruct((padded, width), BF16),
            jax.ShapeDtypeStruct((width // DH, padded, padded), BF16),
        ],
        compiler_params=pltpu.CompilerParams(vmem_limit_bytes=40 * 2**20),
        name="attend_forward",
    )(query_a, query_b, key_rows, value_rows, pos_keys)


def attend_backward(query_a, query_b, key_rows, value_rows, pos_keys, probs, attn_grad):
    padded, width = key_rows.shape
    span = padded + BLOCK

    def kernel(
        qa_ref, qb_ref, k_ref, v_ref, pk_ref, probs_ref, grad_ref,
        dq_ref, dk_ref, dv_ref, dpk_ref, bias_ref,
        dk_acc, dv_acc, dpk_acc,
    ):
        dk_acc[...] = jnp.zeros_like(dk_acc)
        dv_acc[...] = jnp.zeros_like(dv_acc)
        dpk_acc[...] = jnp.zeros_like(dpk_acc)
        row_ids = lax.broadcasted_iota(jnp.int32, (BLOCK, BLOCK), 0)
        col_ids = lax.broadcasted_iota(jnp.int32, (BLOCK, BLOCK), 1)
        flip_f = jnp.where(row_ids + col_ids == BLOCK - 1, 1.0, 0.0)
        flip = flip_f.astype(BF16)

        def one_block(block, sums):
            sum_a, sum_b = sums
            rows = pl.ds(pl.multiple_of(block * BLOCK, BLOCK), BLOCK)
            near = pl.ds(pl.multiple_of(padded - BLOCK - block * BLOCK, BLOCK), span)
            qa, qb, grad = qa_ref[rows, :], qb_ref[rows, :], grad_ref[rows, :]
            qb_flip = matmul(flip, qb).astype(BF16)
            dqa = jnp.zeros((BLOCK, PAIR), F32)
            dqb_flip = jnp.zeros((BLOCK, PAIR), F32)
            for head in range(2):
                mask = head_mask(head, 1.0)
                probs_low = probs_ref[head, rows, :]
                probs_f = probs_low.astype(F32)
                prob_grad = outer_cols(grad * head_mask(head, DH ** (-0.5)), v_ref[...])
                product = probs_f * prob_grad
                centre = jnp.sum(product, axis=-1, keepdims=True)
                score_grad = (product - probs_f * centre).astype(BF16)
                dqa += matmul(score_grad, k_ref[...] * mask)
                dk_acc[...] += inner_rows(qa * mask, score_grad)
                dv_acc[...] += inner_rows(grad * mask, probs_low)
                flipped = matmul(flip, score_grad)
                wide = jnp.concatenate([flipped, jnp.zeros((BLOCK, BLOCK), F32)], axis=1)
                position_grad = pltpu.roll(wide, 0, 1, stride=1, stride_axis=0).astype(BF16)
                dqb_flip += matmul(position_grad, pk_ref[near, :] * mask)
                dpk_acc[:, near] += inner_rows(qb_flip * mask, position_grad)
            dqb = lax.dot_general(
                flip_f, dqb_flip, (((1,), (0,)), ((), ())),
                precision=lax.Precision.HIGHEST, preferred_element_type=F32,
            )
            dq_ref[rows, :] = (dqa + dqb).astype(BF16)
            return (
                sum_a + jnp.sum(dqa, axis=0, keepdims=True),
                sum_b + jnp.sum(dqb_flip, axis=0, keepdims=True),
            )

        start = jnp.zeros((1, PAIR), F32)
        sum_a, sum_b = lax.fori_loop(0, padded // BLOCK, one_block, (start, start))
        bias_ref[...] = jnp.concatenate([sum_a, sum_b, jnp.zeros((6, PAIR), F32)], axis=0)
        dk_ref[...] = dk_acc[...].T.astype(BF16)
        dv_ref[...] = dv_acc[...].T.astype(BF16)
        dpk_ref[...] = dpk_acc[...].T.astype(BF16)

    rows_spec = pl.BlockSpec((padded, PAIR), lambda pair: (0, pair))
    wide_spec = pl.BlockSpec((2 * padded, PAIR), lambda pair: (0, pair))
    return pl.pallas_call(
        kernel,
        grid=(width // PAIR,),
        in_specs=[rows_spec] * 4
        + [wide_spec, pl.BlockSpec((2, padded, padded), lambda pair: (pair, 0, 0)), rows_spec],
        out_specs=[rows_spec] * 3 + [wide_spec, pl.BlockSpec((8, PAIR), lambda pair: (0, pair))],
        out_shape=[jax.ShapeDtypeStruct((padded, width), BF16)] * 3
        + [
            jax.ShapeDtypeStruct((2 * padded, width), BF16),
            jax.ShapeDtypeStruct((8, width), F32),
        ],
        scratch_shapes=[
            pltpu.VMEM((PAIR, padded), F32),
            pltpu.VMEM((PAIR, padded), F32),
            pltpu.VMEM((PAIR, 2 * padded), F32),
        ],
        compiler_params=pltpu.CompilerParams(vmem_limit_bytes=40 * 2**20),
        name="attend_backward",
    )(query_a, query_b, key_rows, value_rows, pos_keys, probs, attn_grad)


ROWS = 64


def depthwise(signal, taps):
    out_rows, width = signal.shape[0] - 32, signal.shape[1]

    def kernel(signal_ref, taps_ref, out_ref):
        def one_chunk(chunk, carry):
            base = pl.multiple_of(chunk * ROWS, ROWS)
            total = jnp.zeros((ROWS, 128), F32)
            for tap in range(31):
                total += signal_ref[pl.ds(base + tap, ROWS), :] * taps_ref[tap : tap + 1, :]
            out_ref[pl.ds(base, ROWS), :] = total
            return carry

        lax.fori_loop(0, out_rows // ROWS, one_chunk, 0)

    return pl.pallas_call(
        kernel,
        grid=(width // 128,),
        in_specs=[
            pl.BlockSpec((out_rows + 32, 128), lambda part: (0, part)),
            pl.BlockSpec((32, 128), lambda part: (0, part)),
        ],
        out_specs=pl.BlockSpec((out_rows, 128), lambda part: (0, part)),
        out_shape=jax.ShapeDtypeStruct((out_rows, width), F32),
        name="depthwise",
    )(signal, taps)


def depthwise_taps(signal, upstream):
    out_rows, width = upstream.shape

    def kernel(signal_ref, up_ref, out_ref):
        def one_chunk(chunk, totals):
            base = pl.multiple_of(chunk * ROWS, ROWS)
            grad = up_ref[pl.ds(base, ROWS), :]
            result = []
            for tap in range(31):
                product = signal_ref[pl.ds(base + tap, ROWS), :] * grad
                result.append(
                    totals[tap] + jnp.sum(product.reshape(ROWS // 8, 8, 128), axis=0)
                )
            return tuple(result)

        start = tuple(jnp.zeros((8, 128), F32) for _ in range(31))
        totals = lax.fori_loop(0, out_rows // ROWS, one_chunk, start)
        for tap in range(31):
            out_ref[tap : tap + 1, :] = jnp.sum(totals[tap], axis=0, keepdims=True)
        out_ref[31:32, :] = jnp.zeros((1, 128), F32)

    return pl.pallas_call(
        kernel,
        grid=(width // 128,),
        in_specs=[
            pl.BlockSpec((out_rows + 32, 128), lambda part: (0, part)),
            pl.BlockSpec((out_rows, 128), lambda part: (0, part)),
        ],
        out_specs=pl.BlockSpec((32, 128), lambda part: (0, part)),
        out_shape=jax.ShapeDtypeStruct((32, width), F32),
        name="depthwise_taps",
    )(signal, upstream)


def local(
    tokens, ff_in, ff_out, att_qkv, att_pos, att_bias, att_out,
    conv_in, conv_depth, conv_out, gains, out_grad,
):
    length, width = tokens.shape
    dp, tp = lax.axis_size("dp"), lax.axis_size("tensor")
    count = dp * tp
    total_rows = length * count
    padded = -(-length // BLOCK) * BLOCK
    piece = width // count
    units = ff_in.shape[3]
    in_rows, half = att_pos.shape[1], att_pos.shape[2]
    bias_heads, bias_width = att_bias.shape[1], att_bias.shape[2]
    heads = bias_heads * tp
    tap_count = conv_depth.shape[1]
    margin = (tap_count - 1) // 2

    def gather(array):
        return lax.all_gather(array, AXES, axis=0)

    def scatter(array):
        return lax.psum_scatter(array, AXES, scatter_dimension=0, tiled=False)

    small = jnp.concatenate(
        [
            gains[0].reshape(-1),
            conv_depth[0].astype(F32).reshape(-1),
            att_bias[0].astype(F32).reshape(-1),
        ]
    )
    ff_first = gather(jnp.concatenate([ff_in[0, 0].T, ff_out[0, 0]], axis=0))
    small = gather(small)
    att_all = gather(
        jnp.concatenate([att_qkv[0].reshape(-1, half), att_pos[0], att_out[0].T], axis=0)
    )
    rest_all = gather(
        jnp.concatenate(
            [
                conv_in[0].transpose(1, 2, 0).reshape(2 * piece, width),
                conv_out[0],
                ff_in[0, 1].T,
                ff_out[0, 1],
            ],
            axis=0,
        )
    )
    gain_end, depth_end = 7 * piece, (7 + tap_count) * piece
    gain_rows = small[:, :gain_end].reshape(count, 7, piece).transpose(1, 0, 2).reshape(7, width)
    taps = (
        small[:, gain_end:depth_end]
        .reshape(count, tap_count, piece)
        .transpose(1, 0, 2)
        .reshape(tap_count, width)
    )
    bias = (
        small[:, depth_end:]
        .reshape(dp, tp, bias_heads, bias_width)
        .transpose(1, 2, 0, 3)
        .reshape(heads, 2 * DH)
    )
    w_in_t = [ff_first[:, :units].reshape(-1, width)]
    w_out = [ff_first[:, units:].reshape(-1, width)]
    att_all = att_all.reshape(dp, tp, 5 * in_rows, half)
    w_qkv = (
        att_all[:, :, : 3 * in_rows]
        .reshape(dp, tp, in_rows, 3, half)
        .transpose(0, 2, 3, 1, 4)
        .reshape(width, 3 * width)
    )
    w_pos = att_all[:, :, 3 * in_rows : 4 * in_rows].transpose(0, 2, 1, 3).reshape(width, width)
    w_aout_t = att_all[:, :, 4 * in_rows :].transpose(0, 2, 1, 3).reshape(width, width)
    w_cin_t = (
        rest_all[:, : 2 * piece]
        .reshape(count, 2, piece, width)
        .transpose(1, 0, 2, 3)
        .reshape(2 * width, width)
    )
    w_cout = rest_all[:, 2 * piece : 3 * piece].reshape(width, width)
    w_in_t.append(rest_all[:, 3 * piece : 3 * piece + units].reshape(-1, width))
    w_out.append(rest_all[:, 3 * piece + units :].reshape(-1, width))

    def mlp_forward(residual, module, gain):
        normed = layer_norm(residual, gain).astype(BF16)
        hidden_pre = outer_cols(normed, w_in_t[module])
        hidden = jax.nn.silu(hidden_pre).astype(BF16)
        return residual + 0.5 * matmul(hidden, w_out[module]), (normed, hidden_pre, hidden)

    def mlp_backward(residual, upstream, stored, module, gain):
        normed, hidden_pre, hidden = stored
        branch_grad = (0.5 * upstream).astype(BF16)
        hidden_grad = outer_cols(branch_grad, w_out[module])
        pre_grad = (hidden_grad * silu_slope(hidden_pre)).astype(BF16)
        out_grad_rows = inner_rows(hidden, branch_grad).astype(BF16)
        in_grad_rows = inner_rows(pre_grad, normed).astype(BF16)
        normed_grad = matmul(pre_grad, w_in_t[module])
        residual_grad, gain_grad = norm_back(residual, gain, normed_grad)
        terms = [
            in_grad_rows.reshape(count, units, width),
            out_grad_rows.reshape(count, units, width),
        ]
        return upstream + residual_grad, terms, gain_grad

    def pad_rows(array):
        return jnp.pad(array, ((0, padded - length), (0, 0)))

    residual_0 = tokens.astype(F32)
    residual_1, first_ff = mlp_forward(residual_0, 0, gain_rows[0])

    att_normed = layer_norm(residual_1, gain_rows[1]).astype(BF16)
    packed = matmul(att_normed, w_qkv)
    query = packed[:, :width]
    query_a = pad_rows((query + bias[:, :DH].reshape(-1)).astype(BF16))
    query_b = pad_rows((query + bias[:, DH:].reshape(-1)).astype(BF16))
    key_rows = pad_rows(packed[:, width : 2 * width].astype(BF16))
    value_rows = pad_rows(packed[:, 2 * width :].astype(BF16))
    pos_table = padded_table(padded, width)
    pos_keys = matmul(pos_table, w_pos).astype(BF16)
    attended, probs = attend_forward(query_a, query_b, key_rows, value_rows, pos_keys, length)
    attended = attended[:length]
    residual_2 = residual_1 + outer_cols(attended, w_aout_t)

    conv_normed = layer_norm(residual_2, gain_rows[2]).astype(BF16)
    gate_pair = outer_cols(conv_normed, w_cin_t)
    value_part, gate = gate_pair[:, :width], jax.nn.sigmoid(gate_pair[:, width:])
    conv_pad = ((margin, padded + 32 - margin - length), (0, 0))
    glu = jnp.pad(value_part * gate, conv_pad)
    taps_pad = jnp.pad(taps, ((0, 32 - tap_count), (0, 0)))
    taps_back = jnp.pad(taps[::-1], ((0, 32 - tap_count), (0, 0)))
    mixed_rows = depthwise(glu, taps_pad)[:length]
    own_mean = jnp.mean(mixed_rows, axis=0)
    own_square = jnp.sum((mixed_rows - own_mean) ** 2, axis=0)
    moments = gather(jnp.stack([own_mean, own_square]))
    mean_vec = jnp.mean(moments[:, 0], axis=0)
    var_vec = (
        jnp.sum(moments[:, 1], axis=0) + length * jnp.sum((moments[:, 0] - mean_vec) ** 2, axis=0)
    ) / total_rows
    inv_std = lax.rsqrt(var_vec + EPS)
    normal_rows = (mixed_rows - mean_vec) * inv_std
    batch_out = normal_rows * gain_rows[5] + gain_rows[6]
    activated = jax.nn.silu(batch_out).astype(BF16)
    residual_3 = residual_2 + matmul(activated, w_cout)

    residual_4, second_ff = mlp_forward(residual_3, 1, gain_rows[3])
    block_out = layer_norm(residual_4, gain_rows[4])

    upstream, final_gain = norm_back(residual_4, gain_rows[4], out_grad)
    upstream, second_terms, second_gain = mlp_backward(
        residual_3, upstream, second_ff, 1, gain_rows[3]
    )
    second_sum = scatter(jnp.concatenate(second_terms, axis=1))

    branch_grad = upstream.astype(BF16)
    act_grad = outer_cols(branch_grad, w_cout)
    cout_terms = inner_rows(activated, branch_grad).astype(BF16).reshape(count, piece, width)
    batch_grad = act_grad * silu_slope(batch_out)
    shift_part = jnp.sum(batch_grad, axis=0)
    scale_part = jnp.sum(batch_grad * normal_rows, axis=0)
    totals = jnp.sum(gather(jnp.stack([scale_part, shift_part])), axis=0)
    mixed_grad = (
        gain_rows[5]
        * inv_std
        * (batch_grad - totals[1] / total_rows - normal_rows * (totals[0] / total_rows))
    )
    mixed_pad = jnp.pad(mixed_grad, conv_pad)
    glu_grad = depthwise(mixed_pad, taps_back)[:length]
    depth_grad = depthwise_taps(glu, pad_rows(mixed_grad))[:tap_count]
    pair_grad = jnp.concatenate(
        [glu_grad * gate, glu_grad * value_part * gate * (1.0 - gate)], axis=1
    ).astype(BF16)
    cin_terms = (
        inner_rows(pair_grad, conv_normed)
        .astype(BF16)
        .reshape(2, count, piece, width)
        .transpose(1, 0, 2, 3)
        .reshape(count, 2 * piece, width)
    )
    conv_sum = scatter(jnp.concatenate([cin_terms, cout_terms], axis=1))
    residual_grad, conv_gain = norm_back(residual_2, gain_rows[2], matmul(pair_grad, w_cin_t))
    upstream = upstream + residual_grad

    branch_grad = upstream.astype(BF16)
    attn_grad = pad_rows(matmul(branch_grad, w_aout_t).astype(BF16))
    aout_terms = inner_rows(branch_grad, attended)
    query_grad, key_grad, value_grad, pos_grad, bias_sums = attend_backward(
        query_a, query_b, key_rows, value_rows, pos_keys, probs, attn_grad
    )
    pack_grad = jnp.concatenate([query_grad, key_grad, value_grad], axis=1)[:length]
    qkv_terms = inner_rows(att_normed, pack_grad)
    pos_terms = inner_rows(pos_table, pos_grad)

    def square_terms(array):
        shaped = array.astype(BF16).reshape(dp, in_rows, tp, half).transpose(0, 2, 1, 3)
        return shaped.reshape(count, in_rows, half)

    qkv_terms = (
        qkv_terms.astype(BF16)
        .reshape(dp, in_rows, 3, tp, half)
        .transpose(0, 3, 1, 2, 4)
        .reshape(count, 3 * in_rows, half)
    )
    att_sum = scatter(
        jnp.concatenate([qkv_terms, square_terms(pos_terms), square_terms(aout_terms)], axis=1)
    )
    residual_grad, attend_gain = norm_back(
        residual_1, gain_rows[1], outer_cols(pack_grad, w_qkv)
    )
    upstream = upstream + residual_grad

    tokens_grad, first_terms, first_gain = mlp_backward(
        residual_0, upstream, first_ff, 0, gain_rows[0]
    )
    first_sum = scatter(jnp.concatenate(first_terms, axis=1))

    gain_terms = jnp.stack(
        [first_gain, attend_gain, conv_gain, second_gain, final_gain, scale_part, shift_part]
    )
    bias_terms = jnp.concatenate(
        [bias_sums[0].reshape(heads, DH), bias_sums[1].reshape(heads, DH)], axis=1
    )
    small_terms = jnp.concatenate(
        [
            gain_terms.reshape(7, count, piece).transpose(1, 0, 2).reshape(count, -1),
            depth_grad.reshape(tap_count, count, piece).transpose(1, 0, 2).reshape(count, -1),
            bias_terms.reshape(tp, bias_heads, dp, bias_width)
            .transpose(2, 0, 1, 3)
            .reshape(count, -1),
        ],
        axis=1,
    )
    small_sum = scatter(small_terms)

    first_sum, second_sum = first_sum.astype(F32), second_sum.astype(F32)
    conv_sum, att_sum = conv_sum.astype(F32), att_sum.astype(F32)
    return (
        block_out,
        tokens_grad,
        jnp.stack([first_sum[:units].T, second_sum[:units].T])[None],
        jnp.stack([first_sum[units:], second_sum[units:]])[None],
        att_sum[: 3 * in_rows].reshape(1, in_rows, 3, half),
        att_sum[3 * in_rows : 4 * in_rows][None],
        small_sum[depth_end:].reshape(1, bias_heads, bias_width),
        att_sum[4 * in_rows :].T[None],
        conv_sum[: 2 * piece].reshape(2, piece, width).transpose(2, 0, 1)[None],
        small_sum[gain_end:depth_end].reshape(1, tap_count, piece),
        conv_sum[2 * piece :][None],
        small_sum[:gain_end].reshape(1, 7, piece),
    )


def solution(mesh):
    placed = (
        P(AXES, None),
        P(None, None, None, AXES),
        P(None, None, AXES, None),
        P(None, "dp", None, "tensor"),
        P(None, "dp", "tensor"),
        P(None, "tensor", "dp"),
        P(None, "tensor", "dp"),
        P(None, None, None, AXES),
        P(None, None, AXES),
        P(None, AXES, None),
        P(None, None, AXES),
        P(AXES, None),
    )
    return jax.shard_map(
        local,
        mesh=mesh,
        in_specs=placed,
        out_specs=(P(AXES, None),) + placed[:11],
        check_vma=False,
    )
```

profile of v0, /device:TPU:0, one launch (start us, length us, event | category | flops | bytes accessed | tf_op | source)
XLA Modules:
  0.0 1136.9 jit_solution(698972968947160314)
XLA Ops:
  14.1 70.4 %all-gather.6 = f32[32,1,640]{2,1,0:T(1,128)S(1)} all-gather(f32[1,1,640]{2,1,0:T(1,128)S(1)} %reshape.460), channel_id=2, replica_groups=mesh['dp'=16,'tensor'=2] {'dp','tensor'}, dimensions={0}, use_global_device_ids=true | all-gather | bytes 84480 | tf_op jit(solution)/shard_map/all_gather | solution.py:275
  96.8 3.9 reshape.415
  101.3 13.6 %convolution_convert_fusion.pk_ref = bf16[1536,512]{1,0:T(8,128)(2,1)} fusion(bf16[512,512]{1,0:T(8,128)(2,1)S(1)} %bitcast.195, f32[512]{0:T(512)S(1)} %fusion.39, f32[1536]{0:T(1024)S(1)} %subtract_convert_fusion, pred[512]{0:T(512)(128)(4,1)S(1)} %fusion.35), kind=kOutput, calls=%fused_computation.12 | convolution fusion | flops 808452096 | bytes 2105856 | tf_op jit(solution)/shard_map/dot_general | solution.py:20
  115.0 22.3 %all-gather.13.cloned.1.call-done = bf16[4096,512]{1,0:T(8,128)(2,1)} async-done(((bf16[128,512]{1,0:T(8,128)(2,1)}), bf16[4096,512]{1,0:T(8,128)(2,1)}) %all-gather.13.cloned.1.call-update) | async-done | bytes 4194320 | tf_op jit(solution)/shard_map/all_gather | solution.py:275
  139.7 4.6 multiply_convert_fusion.3
  149.9 25.2 %attend_forward.1 = (bf16[768,512]{1,0:T(8,128)(2,1)S(1)}, bf16[8,768,768]{2,1,0:T(8,128)(2,1)}) custom-call(bf16[768,512]{1,0:T(8,128)(2,1)S(1)} %pad.34.qa_ref, bf16[768,512]{1,0:T(8,128)(2,1)S(1)} %pad.35.qb_ref, bf16[768,512]{1,0:T(8,128)(2,1)S(1)} %pad.36.k_ref, bf16[768,512]{1,0:T(8,128)(2,1)S(1)} %pad.37.v_ref, bf16[1536,512]{1,0:T(8,128)(2,1)S(1)} %copy-done), custom_call_target="tpu_custom_call" | custom-call | tf_op jit(solution)/shard_map/attend_forward/pallas_call | solution.py:98
  177.5 28.9 %all-gather.17.cloned.1.call-done = bf16[5632,512]{1,0:T(8,128)(2,1)} async-done(((bf16[176,512]{1,0:T(8,128)(2,1)}), bf16[5632,512]{1,0:T(8,128)(2,1)}) %all-gather.17.cloned.1.call-update) | async-done | bytes 5767184 | tf_op jit(solution)/shard_map/all_gather | solution.py:275
  209.6 4.7 fusion.59
  220.2 6.0 depthwise.2
  229.6 67.4 %all-gather.7 = f32[32,2,512]{2,1,0:T(2,128)S(1)} all-gather(f32[1,2,512]{2,1,0:T(2,128)S(1)} %maximum_bitcast_fusion.2), channel_id=6, replica_groups=mesh['dp'=16,'tensor'=2] {'dp','tensor'}, dimensions={0}, use_global_device_ids=true | all-gather | bytes 135168 | tf_op jit(solution)/shard_map/all_gather | solution.py:275
  307.8 2.9 multiply_convert_fusion.1
  316.3 64.0 %all-gather.8 = f32[32,2,512]{2,1,0:T(2,128)S(1)} all-gather(f32[1,2,512]{2,1,0:T(2,128)S(1)} %maximum_bitcast_fusion.3), channel_id=7, replica_groups=mesh['dp'=16,'tensor'=2] {'dp','tensor'}, dimensions={0}, use_global_device_ids=true | all-gather | bytes 135168 | tf_op jit(solution)/shard_map/all_gather | solution.py:275
  385.4 3.5 convolution_convert_fusion.8
  388.9 6.2 depthwise.3
  395.1 3.2 multiply_convert_fusion.6
  404.8 51.9 %attend_backward.1 = (bf16[768,512]{1,0:T(8,128)(2,1)S(1)}, bf16[768,512]{1,0:T(8,128)(2,1)S(1)}, bf16[768,512]{1,0:T(8,128)(2,1)S(1)}, bf16[1536,512]{1,0:T(8,128)(2,1)S(1)}, f32[8,512]{1,0:T(8,128)S(1)}) custom-call(bf16[768,512]{1,0:T(8,128)(2,1)S(1)} %pad.34.qa_ref, bf16[768,512]{1,0:T(8,128)(2,1)S(1)} %pad.35.qb_ref, bf16[768,512]{1,0:T(8,128)(2,1)S(1)} %pad.36.k_ref, ...), custom_call_target="tpu_custom_call" | custom-call | tf_op jit(solution)/shard_map/attend_backward/pallas_call | solution.py:172
  461.7 2.9 multiply_convert_fusion
  464.6 3.0 fusion.16
  468.2 5.9 depthwise_taps.1
  483.9 12.9 %fusion.21 = bf16[512,512]{1,0:T(8,128)(2,1)} fusion(bf16[1536,512]{1,0:T(8,128)(2,1)S(1)} %copy-done.5, f32[512]{0:T(512)S(1)} %fusion.39, f32[1536]{0:T(1024)S(1)} %subtract_convert_fusion, pred[512]{0:T(512)(128)(4,1)S(1)} %fusion.35), kind=kOutput, calls=%fused_computation.96 | convolution fusion | flops 807927808 | bytes 2105856 | tf_op jit(solution)/shard_map/dot_general | solution.py:24
  503.3 4.1 convolution_convert_fusion.1
  507.5 3.6 reshape.432
  511.0 2.9 copy.173
  516.9 3.0 copy.153
  521.3 3.9 convolution_convert_fusion.2
  529.8 4.0 convolution_convert_fusion.5
  538.3 3.1 fusion.15
  541.4 59.2 %all-reduce.13.cloned.1.call-done = f32[32,640]{0,1:T(8,128)} async-done(((f32[32,640]{0,1:T(8,128)}), f32[32,640]{0,1:T(8,128)}) %all-reduce.13.cloned.1.call-update) | async-done | bytes 81936
  605.7 98.8 %reduce-scatter.12.cloned.1.call-done = bf16[1,48,512]{2,1,0:T(8,128)(2,1)} async-done(((bf16[32,48,512]{2,1,0:T(8,128)(2,1)}), bf16[1,48,512]{2,1,0:T(8,128)(2,1)}) %reduce-scatter.12.cloned.1.call-update) | async-done | bytes 49168 | tf_op jit(solution)/shard_map/reduce_scatter | solution.py:278
  707.2 137.5 %reduce-scatter.10.cloned.1.call-done = bf16[1,160,256]{2,1,0:T(8,128)(2,1)} async-done(((bf16[32,160,256]{2,1,0:T(8,128)(2,1)}), bf16[1,160,256]{2,1,0:T(8,128)(2,1)}) %reduce-scatter.10.cloned.1.call-update) | async-done | bytes 81936 | tf_op jit(solution)/shard_map/reduce_scatter | solution.py:278
  849.2 136.1 %reduce-scatter.8.cloned.1.call-done = bf16[1,128,512]{2,1,0:T(8,128)(2,1)} async-done(((bf16[32,128,512]{2,1,0:T(8,128)(2,1)}), bf16[1,128,512]{2,1,0:T(8,128)(2,1)}) %reduce-scatter.8.cloned.1.call-update) | async-done | bytes 131088 | tf_op jit(solution)/shard_map/reduce_scatter | solution.py:278
  986.3 140.3 %reduce-scatter.6.cloned.1.call-done = bf16[1,128,512]{2,1,0:T(8,128)(2,1)} async-done(((bf16[32,128,512]{2,1,0:T(8,128)(2,1)}), bf16[1,128,512]{2,1,0:T(8,128)(2,1)}) %reduce-scatter.6.cloned.1.call-update) | async-done | bytes 131088 | tf_op jit(solution)/shard_map/reduce_scatter | solution.py:278
  (332 shorter events, 121.5 us)
Async XLA Ops:
  7.2 6.5 copy-start.53
  7.2 6.6 copy-start.51
  7.2 6.7 copy-start.52
  7.2 81.6 %all-gather.15.cloned.1.call-start = ((), (), s32[]{:S(2)}) async-start(), calls=%async_computation.9 | async-start | bytes 2703360 | tf_op jit(solution)/shard_map/all_gather | solution.py:275
  9.6 127.7 %all-gather.13.cloned.1.call-start = ((), (), s32[]{:S(2)}) async-start(), calls=%async_computation.8 | async-start | bytes 4325376 | tf_op jit(solution)/shard_map/all_gather | solution.py:275
  12.1 194.4 %all-gather.17.cloned.1.call-start = ((), (), s32[]{:S(2)}) async-start(), calls=%async_computation.10 | async-start | bytes 5947392 | tf_op jit(solution)/shard_map/all_gather | solution.py:275
  13.6 586.9 %all-reduce.13.cloned.1.call-start = ((), (), s32[]{:S(2)}) async-start(), calls=%async_computation.11 | async-start | bytes 655360
  100.7 45.9 %copy-start.24 = (bf16[512,1536]{1,0:T(8,128)(2,1)}, bf16[512,1536]{1,0:T(8,128)(2,1)S(1)}, u32[]{:S(2)}) copy-start(bf16[512,1536]{1,0:T(8,128)(2,1)S(1)} %reshape.415) | copy-start | bytes 4718596
  139.7 4.6 copy-start.41
  139.7 4.6 copy-start.43
  146.2 29.0 %copy-start.12 = (f32[750,512]{1,0:T(8,128)}, f32[750,512]{1,0:T(8,128)S(1)}, u32[]{:S(2)}) copy-start(f32[750,512]{1,0:T(8,128)S(1)} %get-tuple-element.142) | copy-start | bytes 4608004
  149.9 25.2 %copy-start.35 = (bf16[64,8,2,256]{3,1,2,0:T(8,128)(2,1)S(1)}, bf16[64,8,2,256]{3,1,2,0:T(8,128)(2,1)}, u32[]{:S(2)}) copy-start(bf16[64,8,2,256]{3,1,2,0:T(8,128)(2,1)} %copy.170) | copy-start | bytes 1572868
  226.3 71.0 %copy-start.19 = (f32[750,512]{1,0:T(8,128)S(1)}, f32[750,512]{1,0:T(8,128)}, u32[]{:S(2)}) copy-start(f32[750,512]{1,0:T(8,128)} %copy-done.17) | copy-start | bytes 4608004
  226.3 71.0 %copy-start.21 = (f32[768,512]{1,0:T(8,128)S(1)}, f32[768,512]{1,0:T(8,128)}, u32[]{:S(2)}) copy-start(f32[768,512]{1,0:T(8,128)} %depthwise.2) | copy-start | bytes 4718596
  299.2 13.7 %copy-start.33 = (f32[750,512]{1,0:T(8,128)}, f32[750,512]{1,0:T(8,128)S(1)}, u32[]{:S(2)}) copy-start(f32[750,512]{1,0:T(8,128)S(1)} %get-tuple-element.148) | copy-start | bytes 4608004
  307.8 5.1 copy-start.26
  402.9 55.9 %copy-start.15 = (f32[750,512]{1,0:T(8,128)}, f32[750,512]{1,0:T(8,128)S(1)}, u32[]{:S(2)}) copy-start(f32[750,512]{1,0:T(8,128)S(1)} %multiply_add_fusion.1) | copy-start | bytes 4608004
  404.8 51.9 %copy-start.13 = (f32[750,512]{1,0:T(8,128)S(1)}, f32[750,512]{1,0:T(8,128)}, u32[]{:S(2)}) copy-start(f32[750,512]{1,0:T(8,128)} %copy-done.12) | copy-start | bytes 4608004
  404.8 52.0 %copy-start.25 = (bf16[512,1536]{1,0:T(8,128)(2,1)S(1)}, bf16[512,1536]{1,0:T(8,128)(2,1)}, u32[]{:S(2)}) copy-start(bf16[512,1536]{1,0:T(8,128)(2,1)} %copy-done.24) | copy-start | bytes 4718596
  404.8 54.4 %slice-start = ((s8[6160384]{0:T(1024)(128)(4,1)}), s8[1966080]{0:T(1024)(128)(4,1)S(1)}, s32[]{:S(2)}) async-start(s8[6160384]{0:T(1024)(128)(4,1)} %bitcast.214), calls=%async_computation.12 | async-start | bytes 3932160
  456.8 3.9 slice-start.1
  459.3 5.3 copy-start.28
  476.7 227.8 %reduce-scatter.12.cloned.1.call-start = ((), (), s32[]{:S(2)}) async-start(), calls=%async_computation.7 | async-start | bytes 1622016 | tf_op jit(solution)/shard_map/reduce_scatter | solution.py:278
  478.4 366.4 %reduce-scatter.10.cloned.1.call-start = ((), (), s32[]{:S(2)}) async-start(), calls=%async_computation.6 | async-start | bytes 2703360 | tf_op jit(solution)/shard_map/reduce_scatter | solution.py:278
  496.8 6.5 copy-start.7
  496.8 6.5 copy-start.9
  496.8 6.5 copy-start.11
  520.0 465.3 %reduce-scatter.8.cloned.1.call-start = ((), (), s32[]{:S(2)}) async-start(), calls=%async_computation.5 | async-start | bytes 4325376 | tf_op jit(solution)/shard_map/reduce_scatter | solution.py:278
  529.7 4.0 copy-start.29
  529.7 596.9 %reduce-scatter.6.cloned.1.call-start = ((), (), s32[]{:S(2)}) async-start(), calls=%async_computation.4 | async-start | bytes 4325376 | tf_op jit(solution)/shard_map/reduce_scatter | solution.py:278
  529.8 4.0 copy-start.58
  985.3 143.0 %copy-start.48 = (bf16[1,128,512]{2,1,0:T(8,128)(2,1)S(1)}, bf16[1,128,512]{2,1,0:T(8,128)(2,1)}, u32[]{:S(2)}) copy-start(bf16[1,128,512]{2,1,0:T(8,128)(2,1)} %reduce-scatter.8.cloned.1.call-done) | copy-start | bytes 393220
  (38 other events, 83.8 us)
Sparse Core Ops, SparseCore 0:
  11.5 60.9 all-gather.14
  76.1 61.0 all-gather.12
  140.7 65.7 all-gather.16
  476.9 123.6 all-reduce.12
  606.5 98.0 reduce-scatter.11
  706.7 137.9 reduce-scatter.9
  847.1 138.1 reduce-scatter.7
  987.7 138.9 reduce-scatter.5
where the time goes:
time: 1150 us; the launch traced here: 1140 us
  waiting for transfers between devices  623 us (54%)
  blocking collectives  202 us (18%)
  Pallas kernels  95.2 us (8%)
  local copies, waits for them, and re-layouts  84.1 us (7%)
  matrix products  82.2 us (7%)
  other arithmetic  34 us (3%)
  between operations  15.6 us (1%)
    reduce_scatter x4, waiting for transfers between devices, scatter(): return lax.psum_scatter(array, AXES, scatter_dimension=0, tiled=False)  513 us
    all_gather x3, blocking collectives, gather(): return lax.all_gather(array, AXES, axis=0)  202 us
    unnamed x9, waiting for transfers between devices  59.3 us
    pallas_call x1, Pallas kernels, attend_backward(): pl.pallas_call(kernel, grid=(width // PAIR,), in_specs=[rows_spec] * 4 +...  51.9 us
    all_gather x3, waiting for transfers between devices, gather(): return lax.all_gather(array, AXES, axis=0)  51.2 us
    dot_general x9, matrix products, inner_rows(): lax.dot_general(left, right, (((0,), (0,)), ((), ())), preferred_element_...  35.8 us
    dot_general x9, matrix products, matmul(): return jnp.dot(left, right, preferred_element_type=F32)  27.9 us
    pallas_call x1, Pallas kernels, attend_forward(): pl.pallas_call(kernel, grid=(width // PAIR,), in_specs=[rows_spec] * 4 +...  25.2 us
  transfers between devices with their start and end apart: 8, of which 7 were waited for; matrix products, arithmetic and copies ran while one was open for 11% of the time, Pallas kernels for 2%

commit v1 on v0

--- a/solution.py
+++ b/solution.py
@@ -430,7 +430,6 @@
         .transpose(1, 0, 2, 3)
         .reshape(count, 2 * piece, width)
     )
-    conv_sum = scatter(jnp.concatenate([cin_terms, cout_terms], axis=1))
     residual_grad, conv_gain = norm_back(residual_2, gain_rows[2], matmul(pair_grad, w_cin_t))
     upstream = upstream + residual_grad
 
@@ -454,9 +453,9 @@
         .transpose(0, 3, 1, 2, 4)
         .reshape(count, 3 * in_rows, half)
     )
-    att_sum = scatter(
-        jnp.concatenate([qkv_terms, square_terms(pos_terms), square_terms(aout_terms)], axis=1)
-    )
+    att_terms = jnp.concatenate(
+        [qkv_terms, square_terms(pos_terms), square_terms(aout_terms)], axis=1
+    ).reshape(count, -1, width)
     residual_grad, attend_gain = norm_back(
         residual_1, gain_rows[1], outer_cols(pack_grad, w_qkv)
     )
@@ -465,7 +464,6 @@
     tokens_grad, first_terms, first_gain = mlp_backward(
         residual_0, upstream, first_ff, 0, gain_rows[0]
     )
-    first_sum = scatter(jnp.concatenate(first_terms, axis=1))
 
     gain_terms = jnp.stack(
         [first_gain, attend_gain, conv_gain, second_gain, final_gain, scale_part, shift_part]
@@ -483,7 +481,25 @@
         ],
         axis=1,
     )
-    small_sum = scatter(small_terms)
+    small_size = small_terms.shape[1]
+    small_rows = -(-small_size // width)
+    small_terms = jnp.pad(small_terms, ((0, 0), (0, small_rows * width - small_size)))
+    small_terms = small_terms.astype(BF16).reshape(count, small_rows, width)
+    late_terms, second_sum = lax.optimization_barrier(
+        (
+            jnp.concatenate(
+                first_terms + [att_terms, cin_terms, cout_terms, small_terms], axis=1
+            ),
+            second_sum,
+        )
+    )
+    late_sum = scatter(late_terms)
+    conv_start = 2 * units + att_terms.shape[1]
+    small_start = conv_start + 3 * piece
+    first_sum = late_sum[: 2 * units]
+    att_sum = late_sum[2 * units : conv_start].reshape(-1, half)
+    conv_sum = late_sum[conv_start:small_start]
+    small_sum = late_sum[small_start:].astype(F32).reshape(-1)[:small_size]
 
     first_sum, second_sum = first_sum.astype(F32), second_sum.astype(F32)
     conv_sum, att_sum = conv_sum.astype(F32), att_sum.astype(F32)

time: 1150 us -> 719 us (0.63)
  waiting for transfers between devices: 623 us -> 178 us
  local copies, waits for them, and re-layouts: 84.1 us -> 97.5 us
    reduce_scatter x4 -> x2, waiting for transfers between devices: 513 us -> 127 us  [scatter(): return lax.psum_scatter(array, AXES, scatter_dimension=0, tiled=False)]
    unnamed x9 -> x5, waiting for transfers between devices: 59.3 us -> 0.08 us
    unnamed x139 -> x133, local copies, waits for them, and re-layouts: 19.1 us -> 30.9 us
  transfers between devices with their start and end apart: 8 -> 5, of which waited for: 7 -> 3; matrix products, arithmetic and copies ran while one was open for 11% -> 19% of each run, Pallas kernels for 2% -> 12%
where the time goes in v1:
time: 719 us; the launch traced here: 709 us
  blocking collectives  202 us (28%)
  waiting for transfers between devices  178 us (25%)
  local copies, waits for them, and re-layouts  97.5 us (14%)
  Pallas kernels  95.4 us (13%)
  matrix products  85.9 us (12%)
  other arithmetic  34.6 us (5%)
  between operations  15.1 us (2%)
    all_gather x3, blocking collectives, gather(): return lax.all_gather(array, AXES, axis=0)  202 us
    reduce_scatter x2, waiting for transfers between devices, scatter(): return lax.psum_scatter(array, AXES, scatter_dimension=0, tiled=False)  127 us
    pallas_call x1, Pallas kernels, attend_backward(): pl.pallas_call(kernel, grid=(width // PAIR,), in_specs=[rows_spec] * 4 +...  52.1 us
    all_gather x3, waiting for transfers between devices, gather(): return lax.all_gather(array, AXES, axis=0)  51.2 us
    dot_general x9, matrix products, inner_rows(): lax.dot_general(left, right, (((0,), (0,)), ((), ())), preferred_element_...  34.2 us
    unnamed x133, local copies, waits for them, and re-layouts  30.9 us
    dot_general x9, matrix products, matmul(): return jnp.dot(left, right, preferred_element_type=F32)  28.8 us
    pallas_call x1, Pallas kernels, attend_forward(): pl.pallas_call(kernel, grid=(width // PAIR,), in_specs=[rows_spec] * 4 +...  25.3 us
  transfers between devices with their start and end apart: 5, of which 3 were waited for; matrix products, arithmetic and copies ran while one was open for 19% of the time, Pallas kernels for 12%

profile of v1, /device:TPU:0, one launch (start us, length us, event | category | flops | bytes accessed | tf_op | source)
XLA Modules:
  0.0 708.6 jit_solution(5980927214027128939)
XLA Ops:
  14.1 70.4 %all-gather.6 = f32[32,1,640]{2,1,0:T(1,128)S(1)} all-gather(f32[1,1,640]{2,1,0:T(1,128)S(1)} %reshape.482), channel_id=2, replica_groups=mesh['dp'=16,'tensor'=2] {'dp','tensor'}, dimensions={0}, use_global_device_ids=true | all-gather | bytes 84480 | tf_op jit(solution)/shard_map/all_gather | solution.py:275
  96.8 3.9 reshape.435
  101.3 13.6 %convolution_convert_fusion.pk_ref = bf16[1536,512]{1,0:T(8,128)(2,1)} fusion(bf16[512,512]{1,0:T(8,128)(2,1)S(1)} %bitcast.193, f32[512]{0:T(512)S(1)} %fusion.44, f32[1536]{0:T(1024)S(1)} %subtract_convert_fusion, pred[512]{0:T(512)(128)(4,1)S(1)} %fusion.40), kind=kOutput, calls=%fused_computation.11 | convolution fusion | flops 808452096 | bytes 2105856 | tf_op jit(solution)/shard_map/dot_general | solution.py:20
  115.0 22.2 %all-gather.13.cloned.1.call-done = bf16[4096,512]{1,0:T(8,128)(2,1)} async-done(((bf16[128,512]{1,0:T(8,128)(2,1)}), bf16[4096,512]{1,0:T(8,128)(2,1)}) %all-gather.13.cloned.1.call-update) | async-done | bytes 4194320 | tf_op jit(solution)/shard_map/all_gather | solution.py:275
  139.7 4.5 multiply_convert_fusion.3
  149.9 25.3 %attend_forward.1 = (bf16[768,512]{1,0:T(8,128)(2,1)S(1)}, bf16[8,768,768]{2,1,0:T(8,128)(2,1)}) custom-call(bf16[768,512]{1,0:T(8,128)(2,1)S(1)} %pad.39.qa_ref, bf16[768,512]{1,0:T(8,128)(2,1)S(1)} %pad.40.qb_ref, bf16[768,512]{1,0:T(8,128)(2,1)S(1)} %pad.41.k_ref, bf16[768,512]{1,0:T(8,128)(2,1)S(1)} %pad.42.v_ref, bf16[1536,512]{1,0:T(8,128)(2,1)S(1)} %copy-done), custom_call_target="tpu_custom_call" | custom-call | tf_op jit(solution)/shard_map/attend_forward/pallas_call | solution.py:98
  177.6 28.9 %all-gather.17.cloned.1.call-done = bf16[5632,512]{1,0:T(8,128)(2,1)} async-done(((bf16[176,512]{1,0:T(8,128)(2,1)}), bf16[5632,512]{1,0:T(8,128)(2,1)}) %all-gather.17.cloned.1.call-update) | async-done | bytes 5767184 | tf_op jit(solution)/shard_map/all_gather | solution.py:275
  209.7 4.8 fusion.64
  220.4 6.0 depthwise.2
  229.7 67.4 %all-gather.7 = f32[32,2,512]{2,1,0:T(2,128)S(1)} all-gather(f32[1,2,512]{2,1,0:T(2,128)S(1)} %maximum_bitcast_fusion.2), channel_id=6, replica_groups=mesh['dp'=16,'tensor'=2] {'dp','tensor'}, dimensions={0}, use_global_device_ids=true | all-gather | bytes 135168 | tf_op jit(solution)/shard_map/all_gather | solution.py:275
  307.9 3.3 convolution_convert_fusion.1
  311.2 3.1 multiply_convert_fusion.1
  316.5 3.3 convolution_convert_fusion.2
  323.1 64.0 %all-gather.8 = f32[32,2,512]{2,1,0:T(2,128)S(1)} all-gather(f32[1,2,512]{2,1,0:T(2,128)S(1)} %maximum_bitcast_fusion.3), channel_id=7, replica_groups=mesh['dp'=16,'tensor'=2] {'dp','tensor'}, dimensions={0}, use_global_device_ids=true | all-gather | bytes 135168 | tf_op jit(solution)/shard_map/all_gather | solution.py:275
  392.0 6.0 depthwise.3
  398.0 3.2 multiply_convert_fusion.6
  407.1 2.9 multiply_add_fusion.1
  421.6 52.1 %attend_backward.1 = (bf16[768,512]{1,0:T(8,128)(2,1)S(1)}, bf16[768,512]{1,0:T(8,128)(2,1)S(1)}, bf16[768,512]{1,0:T(8,128)(2,1)S(1)}, bf16[1536,512]{1,0:T(8,128)(2,1)S(1)}, f32[8,512]{1,0:T(8,128)S(1)}) custom-call(bf16[768,512]{1,0:T(8,128)(2,1)S(1)} %pad.39.qa_ref, bf16[768,512]{1,0:T(8,128)(2,1)S(1)} %pad.40.qb_ref, bf16[768,512]{1,0:T(8,128)(2,1)S(1)} %pad.41.k_ref, ...), custom_call_target="tpu_custom_call" | custom-call | tf_op jit(solution)/shard_map/attend_backward/pallas_call | solution.py:172
  476.4 12.7 %fusion.21 = bf16[512,512]{1,0:T(8,128)(2,1)} fusion(bf16[1536,512]{1,0:T(8,128)(2,1)S(1)} %get-tuple-element.26, f32[512]{0:T(512)S(1)} %fusion.44, f32[1536]{0:T(1024)S(1)} %subtract_convert_fusion, pred[512]{0:T(512)(128)(4,1)S(1)} %fusion.40), kind=kOutput, calls=%fused_computation.94 | convolution fusion | flops 807927808 | bytes 2105856 | tf_op jit(solution)/shard_map/dot_general | solution.py:24
  491.6 4.2 convolution_convert_fusion.3
  495.8 4.6 reshape.450
  500.4 4.4 copy.141
  504.8 3.7 reshape.451
  510.4 3.0 copy.121
  513.4 5.1 reshape.456
  522.9 5.9 depthwise_taps.1
  530.1 3.8 multiply_reduce_fusion.3
  535.5 5.1 multiply_convert_fusion
  540.7 3.0 fusion.16
  544.7 3.8 convolution_convert_fusion.5
  561.7 3.1 fusion.15
  564.8 126.8 %reduce-scatter.5.cloned.1.call-done = bf16[1,258,512]{2,1,0:T(8,128)(2,1)} async-done(((bf16[32,258,512]{2,1,0:T(8,128)(2,1)}), bf16[1,258,512]{2,1,0:T(8,128)(2,1)}) %reduce-scatter.5.cloned.1.call-update) | async-done | bytes 264208 | tf_op jit(solution)/shard_map/reduce_scatter | solution.py:278
  (323 shorter events, 119.2 us)
Async XLA Ops:
  7.2 6.5 copy-start.52
  7.2 6.6 copy-start.50
  7.2 6.7 copy-start.51
  7.2 81.6 %all-gather.15.cloned.1.call-start = ((), (), s32[]{:S(2)}) async-start(), calls=%async_computation.5 | async-start | bytes 2703360 | tf_op jit(solution)/shard_map/all_gather | solution.py:275
  9.6 127.7 %all-gather.13.cloned.1.call-start = ((), (), s32[]{:S(2)}) async-start(), calls=%async_computation.4 | async-start | bytes 4325376 | tf_op jit(solution)/shard_map/all_gather | solution.py:275
  12.1 194.4 %all-gather.17.cloned.1.call-start = ((), (), s32[]{:S(2)}) async-start(), calls=%async_computation.6 | async-start | bytes 5947392 | tf_op jit(solution)/shard_map/all_gather | solution.py:275
  13.6 548.0 %reduce-scatter.3.cloned.1.call-start = ((), (), s32[]{:S(2)}) async-start(), calls=%async_computation.2 | async-start | bytes 4325376 | tf_op jit(solution)/shard_map/reduce_scatter | solution.py:278
  84.5 3.7 copy-start.25
  100.7 45.8 %copy-start.27 = (bf16[512,1536]{1,0:T(8,128)(2,1)}, bf16[512,1536]{1,0:T(8,128)(2,1)S(1)}, u32[]{:S(2)}) copy-start(bf16[512,1536]{1,0:T(8,128)(2,1)S(1)} %reshape.435) | copy-start | bytes 4718596
  139.7 4.5 copy-start.37
  139.7 4.5 copy-start.39
  146.1 29.1 %copy-start.11 = (f32[750,512]{1,0:T(8,128)}, f32[750,512]{1,0:T(8,128)S(1)}, u32[]{:S(2)}) copy-start(f32[750,512]{1,0:T(8,128)S(1)} %get-tuple-element.142) | copy-start | bytes 4608004
  149.9 25.3 %copy-start.31 = (bf16[64,8,2,256]{3,1,2,0:T(8,128)(2,1)S(1)}, bf16[64,8,2,256]{3,1,2,0:T(8,128)(2,1)}, u32[]{:S(2)}) copy-start(bf16[64,8,2,256]{3,1,2,0:T(8,128)(2,1)} %copy.137) | copy-start | bytes 1572868
  214.6 2.7 copy-start.34
  226.4 71.0 %copy-start.18 = (f32[750,512]{1,0:T(8,128)S(1)}, f32[750,512]{1,0:T(8,128)}, u32[]{:S(2)}) copy-start(f32[750,512]{1,0:T(8,128)} %copy-done.16) | copy-start | bytes 4608004
  226.4 71.0 %copy-start.20 = (f32[768,512]{1,0:T(8,128)S(1)}, f32[768,512]{1,0:T(8,128)}, u32[]{:S(2)}) copy-start(f32[768,512]{1,0:T(8,128)} %depthwise.2) | copy-start | bytes 4718596
  398.0 3.2 copy-start.19
  398.0 3.2 copy-start.35
  401.3 3.3 copy-start.44
  407.0 284.6 %reduce-scatter.5.cloned.1.call-start = ((), (), s32[]{:S(2)}) async-start(), calls=%async_computation.3 | async-start | bytes 8921088 | tf_op jit(solution)/shard_map/reduce_scatter | solution.py:278
  407.0 2.9 copy-start.32
  409.9 4.2 copy-start.14
  504.8 3.7 copy-start.36
  513.4 5.1 copy-start.46
  530.1 3.8 copy-start.12
  530.1 3.8 copy-start.15
  535.5 5.1 copy-start.26
  535.5 5.1 copy-start.38
  540.6 3.0 copy-start.55
  548.5 2.6 copy-start.54
  555.6 2.7 copy-start.30
  561.7 3.1 copy-start.49
  (29 other events, 51.3 us)
Sparse Core Ops, SparseCore 0:
  11.5 60.9 all-gather.14
  76.1 61.0 all-gather.12
  140.7 65.7 all-gather.16
  407.1 140.1 reduce-scatter.2
  561.8 129.8 reduce-scatter.4
